TPU v7x, 256 devices: a whole 4x4x8 slice. The times are simulated.
256 devices in a mesh: gx: 32 (over z, x), gy: 8 (over y, core).
Axes of the slice: x: 4, y: 4, z: 8, core: 2. Of those that a mesh axis runs over, the one named last changes fastest.
Arguments:
- phase_label: int32 [512, 256, 128], P('gx', 'gy'), may hold values from 0 to 2
- tab_index: int32 [512, 256, 128], P('gx', 'gy'), may hold values from 0 to 63
- source_field: float32 [512, 256, 128], P('gx', 'gy'), may hold values from -8 to 8
- sigma_table: float32 [3], replicated, may hold values from 0.2 to 5
- pattern_gain: float32 [16, 64], replicated, may hold values from -6 to 6
Outputs:
- solution: float32 [16, 512, 256, 128], P(None, 'gx', 'gy')
- residual: float32 [16, 512, 256, 128], P(None, 'gx', 'gy')
All inputs are finite; a program needn't handle non-finite values.
Results may differ from a plain program's by a relative error of at most 0.0003.
Values sent between devices are 32-bit elements; how exact they have to be, the bound alone decides.
A program may use at most 192 MiB of HBM per device.

v0:
```python
import jax
import jax.numpy as jnp
import numpy as np
from jax import lax
from jax.sharding import PartitionSpec as P

S = 4
NRHS = 16
TABS = 64
OFFSETS = ((-1, 0, 0), (1, 0, 0), (0, -1, 0), (0, 1, 0), (0, 0, -1), (0, 0, 1))


def with_halo(value, sides, width):
    for axis, dim in sides:
        size, length = (lax.axis_size(axis), value.shape[dim])
        up = [(i, (i + 1) % size) for i in range(size - 1)]
        down = [(j, i) for i, j in up]
        last = lax.slice_in_dim(value, length - width, length, axis=dim)
        initial = lax.slice_in_dim(value, 0, width, axis=dim)
        before = lax.ppermute(last, axis, up)
        after = lax.ppermute(initial, axis, down)
        value = jnp.concatenate([before, value, after], axis=dim)
    return value


def moved(array, a, b, c):
    sx = array.shape[-3]
    sy = array.shape[-2]
    sz = array.shape[-1]
    return array[..., 1 + a : sx - 1 + a, 1 + b : sy - 1 + b, 1 + c : sz - 1 + c]


def neighbour_mean(fields, conduct):
    fields_z = jnp.pad(fields, ((0, 0), (0, 0), (0, 0), (1, 1)))
    conduct_z = jnp.pad(conduct, ((0, 0), (0, 0), (1, 1)))
    centre = moved(conduct_z, 0, 0, 0)
    summed = jnp.zeros(fields.shape[:1] + centre.shape, jnp.float32)
    weights = jnp.zeros(centre.shape, jnp.float32)
    for offset in OFFSETS:
        face = 0.5 * (centre + moved(conduct_z, offset[0], offset[1], offset[2]))
        summed = summed + face[None] * moved(fields_z, offset[0], offset[1], offset[2])
        weights = weights + face
    inside = centre > 0
    return jnp.where(inside[None], summed / jnp.where(inside, weights, 1.0)[None], 0.0)


def difference_matrix():
    matrix = np.zeros((NRHS * (S + 1), NRHS * S), np.float32)
    for step in range(S):
        for column in range(NRHS):
            matrix[step * NRHS + column, step * NRHS + column] = 1.0
            matrix[(step + 1) * NRHS + column, step * NRHS + column] = -1.0
    return jnp.asarray(matrix)


def least_squares(gram):
    highest = lax.Precision.HIGHEST
    diff = difference_matrix()
    hess = jnp.dot(diff.T, jnp.dot(gram, diff, precision=highest), precision=highest)
    right_block = jnp.dot(diff.T, gram[:, :NRHS], precision=highest)
    factor = jnp.linalg.cholesky(hess)
    coeffs = jax.scipy.linalg.cho_solve((factor, True), right_block)
    return (diff, coeffs)


def shards(phase_label, tab_index, source_field, sigma_table, pattern_gain):
    highest = lax.Precision.HIGHEST
    shape = phase_label.shape
    conduct = jnp.where(
        phase_label == 0,
        sigma_table[0],
        jnp.where(phase_label == 1, sigma_table[1], sigma_table[2]),
    )
    onehot = (tab_index.reshape(1, -1) == jnp.arange(TABS, dtype=jnp.int32)[:, None]).astype(
        jnp.float32
    )
    start = jnp.dot(pattern_gain, onehot, precision=highest) * source_field.reshape(1, -1)
    start = start.reshape((NRHS,) + shape)
    stacked = jnp.concatenate([conduct[None], start], 0)
    krylov = [start]
    ghosted = with_halo(stacked, (("gx", 1), ("gy", 2)), 1)
    conduct_wide = ghosted[0]
    current = neighbour_mean(ghosted[1:], conduct_wide)
    krylov.append(current)
    for step in range(S - 1):
        padded = with_halo(current, (("gx", 1), ("gy", 2)), 1)
        current = neighbour_mean(padded, conduct_wide)
        krylov.append(current)
    flat = jnp.concatenate([field.reshape(NRHS, -1) for field in krylov], 0)
    gram = lax.psum(jnp.dot(flat, flat.T, precision=highest), ("gx", "gy"))
    diff, coeffs = least_squares(gram)
    solution = jnp.dot(coeffs.T, flat[: S * NRHS], precision=highest)
    combined = jnp.dot(diff, coeffs, precision=highest)
    residual = flat[:NRHS] - jnp.dot(combined.T, flat, precision=highest)
    return (solution.reshape((NRHS,) + shape), residual.reshape((NRHS,) + shape))


def solution(mesh):
    placed = (P("gx", "gy", None), P("gx", "gy", None), P("gx", "gy", None), P(), P())
    return jax.shard_map(
        shards,
        mesh=mesh,
        in_specs=placed,
        out_specs=(P(None, "gx", "gy", None), P(None, "gx", "gy", None)),
        check_vma=False,
    )
```

profile of v0, /device:TPU:1, one launch (start us, length us, event | category | flops | bytes accessed | tf_op | source)
XLA Modules:
  0.0 357.0 jit_solution(16355060055221915815)
XLA Ops:
  2.1 7.5 %constant_dynamic-update-slice_fusion.3 = (f32[80,65536]{1,0:T(8,128)}, f32[65536,16]{0,1:T(8,128)S(1)}) fusion(f32[65536]{0:T(1024)} %bitcast.93, f32[16,64]{1,0:T(8,128)S(1)} %copy-done, s32[65536]{0:T(1024)} %bitcast.94), kind=kOutput, calls=%fused_computation.175 | convolution fusion | flops 810549248 | bytes 8916992 | tf_op jit(solution)/shard_map/dot_general | solution.py:77
  18.9 4.0 %collective-permute-done = f32[17,1,32,128]{3,2,1,0:T(8,128)S(1)} collective-permute-done((f32[17,1,32,128]{3,2,1,0:T(8,128)S(1)}, f32[17,1,32,128]{3,2,1,0:T(8,128)S(1)}, u32[]{:S(2)}, u32[]{:S(2)}) %collective-permute-start) | collective-permute-done | bytes 278560 | tf_op jit(solution)/shard_map/ppermute | solution.py:20
  26.9 5.0 %collective-permute-start.2 = (f32[17,18,1,128]{3,2,1,0:T(1,128)S(1)}, f32[17,18,1,128]{3,2,1,0:T(1,128)S(1)}, u32[]{:S(2)}, u32[]{:S(2)}) collective-permute-start(f32[17,18,1,128]{3,2,1,0:T(1,128)S(1)} %get-tuple-element.10), channel_id=1, source_target_pairs={{0,1},{1,2},{2,3},{3,4},{4,5},{5,6},{6,7},{8,9},{9,10},{10,11},{11... | collective-permute-start | bytes 470024 | tf_op jit(solution)/shard_map/ppermute | solution.py:20
  34.1 4.4 %collective-permute-done.3 = f32[17,18,1,128]{3,2,1,0:T(1,128)S(1)} collective-permute-done((f32[17,18,1,128]{3,2,1,0:T(1,128)S(1)}, f32[17,18,1,128]{3,2,1,0:T(1,128)S(1)}, u32[]{:S(2)}, u32[]{:S(2)}) %collective-permute-start.3) | collective-permute-done | bytes 156704 | tf_op jit(solution)/shard_map/ppermute | solution.py:21
  39.7 9.6 %select_maximum_fusion.12 = f32[16,18,34,130]{3,2,1,0:T(8,128)} fusion(f32[17,18,1,128]{3,2,1,0:T(1,128)S(1)} %collective-permute-done.3, f32[17,18,1,128]{3,2,1,0:T(1,128)S(1)} %collective-permute-done.2, f32[17,1,32,128]{3,2,1,0:T(8,128)S(1)} %collective-permute-done.1, f32[17,1,32,128]{3,2,1,0:T(8,128)S(1)} %collective-permute-done, ...), kind=kLoop, calls=%fused_computation.25 | loop fusion | flops 17821440 | bytes 10418688 | tf_op jit(solution)/shard_map/concatenate | solution.py:22
  49.3 9.0 %fusion.45 = f32[16,16,32,128]{3,2,1,0:T(8,128)S(1)} fusion(f32[16,18,34,130]{3,2,1,0:T(8,128)} %select_maximum_fusion.12, f32[17,18,1,128]{3,2,1,0:T(1,128)} %copy-done.13, f32[17,1,32,128]{3,2,1,0:T(8,128)} %copy-done.9, f32[17,1,32,128]{3,2,1,0:T(8,128)} %copy-done.8, f32[16,16,32,128]{3,2,1,0:T(8,128)S(1)} %bitcast.84, ...), kind=kLoop, calls=%fused_computation.102 | loop fusion | flops 26214400 | bytes 19810304 | tf_op jit(solution)/shard_map/jit(_where)/select_n | solution.py:44
  64.8 4.1 %collective-permute-done.5 = f32[16,1,32,128]{3,2,1,0:T(8,128)S(1)} collective-permute-done((f32[16,1,32,128]{3,2,1,0:T(8,128)S(1)}, f32[16,1,32,128]{3,2,1,0:T(8,128)S(1)}, u32[]{:S(2)}, u32[]{:S(2)}) %collective-permute-start.5) | collective-permute-done | bytes 262176 | tf_op jit(solution)/shard_map/ppermute | solution.py:21
  69.1 5.2 %collective-permute-start.6 = (f32[16,18,1,128]{3,2,1,0:T(1,128)S(1)}, f32[16,18,1,128]{3,2,1,0:T(1,128)S(1)}, u32[]{:S(2)}, u32[]{:S(2)}) collective-permute-start(f32[16,18,1,128]{3,2,1,0:T(1,128)S(1)} %get-tuple-element.16), channel_id=1, source_target_pairs={{0,1},{1,2},{2,3},{3,4},{4,5},{5,6},{6,7},{8,9},{9,10},{10,11},{11... | collective-permute-start | bytes 442376 | tf_op jit(solution)/shard_map/ppermute | solution.py:20
  76.6 4.4 %collective-permute-done.7 = f32[16,18,1,128]{3,2,1,0:T(1,128)S(1)} collective-permute-done((f32[16,18,1,128]{3,2,1,0:T(1,128)S(1)}, f32[16,18,1,128]{3,2,1,0:T(1,128)S(1)}, u32[]{:S(2)}, u32[]{:S(2)}) %collective-permute-start.7) | collective-permute-done | bytes 147488 | tf_op jit(solution)/shard_map/ppermute | solution.py:21
  80.9 8.9 %select_maximum_fusion.8 = f32[16,18,34,130]{3,2,1,0:T(8,128)} fusion(f32[16,18,1,128]{3,2,1,0:T(1,128)S(1)} %collective-permute-done.7, f32[16,18,1,128]{3,2,1,0:T(1,128)S(1)} %collective-permute-done.6, f32[16,1,32,128]{3,2,1,0:T(8,128)S(1)} %collective-permute-done.5, f32[16,16,32,128]{3,2,1,0:T(8,128)S(1)} %fusion.45, ...), kind=kLoop, calls=%fused_computation.21 | loop fusion | flops 15275520 | bytes 10105344 | tf_op jit(solution)/shard_map/concatenate | solution.py:22
  89.8 10.9 %fusion.34 = f32[16,16,32,128]{3,2,1,0:T(8,128)S(1)} fusion(f32[16,18,34,130]{3,2,1,0:T(8,128)} %select_maximum_fusion.8, f32[16,18,1,128]{3,2,1,0:T(1,128)S(1)} %collective-permute-done.7, f32[16,1,32,128]{3,2,1,0:T(8,128)S(1)} %collective-permute-done.5, f32[16,16,32,128]{3,2,1,0:T(8,128)S(1)} %fusion.45, ...), kind=kLoop, calls=%fused_computation.81 | loop fusion | flops 22020096 | bytes 19496960 | tf_op jit(solution)/shard_map/jit(_where)/select_n | solution.py:44
  100.7 4.4 %collective-permute-start.8 = (f32[16,1,32,128]{3,2,1,0:T(8,128)S(1)}, f32[16,1,32,128]{3,2,1,0:T(8,128)S(1)}, u32[]{:S(2)}, u32[]{:S(2)}) collective-permute-start(f32[16,1,32,128]{3,2,1,0:T(8,128)S(1)} %get-tuple-element.22), channel_id=1, source_target_pairs={{0,8},{8,16},{16,24},{24,32},{32,40},{40,48},{48,56},{56,64},{64,7... | collective-permute-start | bytes 786440 | tf_op jit(solution)/shard_map/ppermute | solution.py:20
  108.5 4.4 %collective-permute-done.9 = f32[16,1,32,128]{3,2,1,0:T(8,128)S(1)} collective-permute-done((f32[16,1,32,128]{3,2,1,0:T(8,128)S(1)}, f32[16,1,32,128]{3,2,1,0:T(8,128)S(1)}, u32[]{:S(2)}, u32[]{:S(2)}) %collective-permute-start.9) | collective-permute-done | bytes 262176 | tf_op jit(solution)/shard_map/ppermute | solution.py:21
  113.2 4.5 %collective-permute-start.10 = (f32[16,18,1,128]{3,2,1,0:T(1,128)S(1)}, f32[16,18,1,128]{3,2,1,0:T(1,128)S(1)}, u32[]{:S(2)}, u32[]{:S(2)}) collective-permute-start(f32[16,18,1,128]{3,2,1,0:T(1,128)S(1)} %get-tuple-element.14), channel_id=1, source_target_pairs={{0,1},{1,2},{2,3},{3,4},{4,5},{5,6},{6,7},{8,9},{9,10},{10,11},{11... | collective-permute-start | bytes 442376 | tf_op jit(solution)/shard_map/ppermute | solution.py:20
  119.8 4.5 %constant_dynamic-update-slice_fusion.2 = f32[80,65536]{1,0:T(8,128)} fusion(f32[80,65536]{1,0:T(8,128)} %get-tuple-element.29, f32[2,8,512,128]{3,2,1,0:T(8,128)S(1)} %bitcast.74), kind=kLoop, calls=%fused_computation.174 | loop fusion | bytes 8388608
  124.3 4.4 %copy.28 = f32[2,8,512,128]{3,1,2,0:T(8,128)} copy(f32[2,8,512,128]{3,2,1,0:T(8,128)S(1)} %bitcast.75) | data formatting | bytes 8388608
  130.0 8.9 %select_maximum_fusion.4 = f32[16,18,34,130]{3,2,1,0:T(8,128)} fusion(f32[16,18,1,128]{3,2,1,0:T(1,128)S(1)} %collective-permute-done.11, f32[16,18,1,128]{3,2,1,0:T(1,128)S(1)} %collective-permute-done.10, f32[16,1,32,128]{3,2,1,0:T(8,128)S(1)} %collective-permute-done.9, f32[16,16,32,128]{3,2,1,0:T(8,128)S(1)} %fusion.34, ...), kind=kLoop, calls=%fused_computation.17 | loop fusion | flops 15275520 | bytes 10105344 | tf_op jit(solution)/shard_map/concatenate | solution.py:22
  138.8 8.1 %fusion.23 = f32[16,16,32,128]{3,2,1,0:T(8,128)S(1)} fusion(f32[16,18,34,130]{3,2,1,0:T(8,128)} %select_maximum_fusion.4, f32[16,18,1,128]{3,2,1,0:T(1,128)} %copy-done.16, f32[16,1,32,128]{3,2,1,0:T(8,128)} %copy-done.11, f32[16,16,32,128]{3,2,1,0:T(8,128)S(1)} %fusion.34, f32[16,1,32,128]{3,2,1,0:T(8,128)} %copy-done.10, f32[16,18,1,128]{3,2,1,0:T(1,128)} %copy-done.15, ...), kind=kLoop, calls=%fused_computation.60 | loop fusion | flops 22020096 | bytes 19496960 | tf_op jit(solution)/shard_map/jit(_where)/select_n | solution.py:44
  152.5 4.4 %constant_dynamic-update-slice_fusion.1 = f32[80,65536]{1,0:T(8,128)} fusion(f32[80,65536]{1,0:T(8,128)} %constant_dynamic-update-slice_fusion.2, f32[2,8,512,128]{3,2,1,0:T(8,128)S(1)} %bitcast.76), kind=kLoop, calls=%fused_computation.173 | loop fusion | bytes 8388608
  157.0 4.4 %copy.27 = f32[2,8,512,128]{3,1,2,0:T(8,128)} copy(f32[2,8,512,128]{3,2,1,0:T(8,128)S(1)} %bitcast.77) | data formatting | bytes 8388608
  167.4 4.4 %constant_dynamic-update-slice_fusion = f32[80,65536]{1,0:T(8,128)} fusion(f32[80,65536]{1,0:T(8,128)} %constant_dynamic-update-slice_fusion.1, f32[2,8,512,128]{3,2,1,0:T(8,128)S(1)} %bitcast.78), kind=kLoop, calls=%fused_computation.172 | loop fusion | bytes 8388608
  171.8 4.4 %copy.26 = f32[2,8,512,128]{3,1,2,0:T(8,128)} copy(f32[2,8,512,128]{3,2,1,0:T(8,128)S(1)} %bitcast.79) | data formatting | bytes 8388608
  176.2 9.0 %select_maximum_fusion = f32[16,18,34,130]{3,2,1,0:T(8,128)} fusion(f32[16,18,1,128]{3,2,1,0:T(1,128)S(1)} %collective-permute-done.15, f32[16,18,1,128]{3,2,1,0:T(1,128)S(1)} %collective-permute-done.14, f32[16,1,32,128]{3,2,1,0:T(8,128)S(1)} %collective-permute-done.13, f32[16,16,32,128]{3,2,1,0:T(8,128)S(1)} %fusion.23, ...), kind=kLoop, calls=%fused_computation.13 | loop fusion | flops 15275520 | bytes 10105344 | tf_op jit(solution)/shard_map/concatenate | solution.py:22
  185.2 10.9 %fusion.12 = f32[16,16,32,128]{3,2,1,0:T(8,128)S(1)} fusion(f32[16,18,34,130]{3,2,1,0:T(8,128)} %select_maximum_fusion, f32[16,18,1,128]{3,2,1,0:T(1,128)S(1)} %collective-permute-done.15, f32[16,1,32,128]{3,2,1,0:T(8,128)S(1)} %collective-permute-done.13, f32[16,16,32,128]{3,2,1,0:T(8,128)S(1)} %fusion.23, ...), kind=kLoop, calls=%fused_computation.39 | loop fusion | flops 22020096 | bytes 19496960 | tf_op jit(solution)/shard_map/jit(_where)/select_n | solution.py:44
  196.1 4.4 %bitcast_dynamic-update-slice_fusion = f32[80,65536]{1,0:T(8,128)} fusion(f32[80,65536]{1,0:T(8,128)} %constant_dynamic-update-slice_fusion, f32[2,8,512,128]{3,2,1,0:T(8,128)S(1)} %bitcast.87), kind=kLoop, calls=%fused_computation.32 | loop fusion | bytes 8388608 | tf_op jit(solution)/shard_map/concatenate | solution.py:89
  200.5 23.0 %fusion.85 = f32[80,80]{1,0:T(8,128)S(1)} fusion(f32[80,65536]{1,0:T(8,128)} %bitcast_dynamic-update-slice_fusion), kind=kOutput, calls=%fused_computation.182 | convolution fusion | flops 5033164800 | bytes 20997120 | tf_op jit(solution)/shard_map/dot_general | solution.py:90
  223.5 85.6 %psum.7 = f32[80,80]{1,0:T(8,128)S(1)} all-reduce(f32[80,80]{1,0:T(8,128)S(1)} %fusion.85), channel_id=1, replica_groups=mesh['gx'=32,'gy'=8] {'gx','gy'}, use_global_device_ids=true, to_apply=%region_0.1 | all-reduce | flops 6400 | bytes 51200 | tf_op jit(solution)/shard_map/psum | solution.py:90
  309.9 5.8 %cholesky.16 = f32[64,64]{1,0:T(8,128)S(1)} custom-call(f32[64,64]{1,0:T(8,128)S(1)} %fusion.73), custom_call_target="Cholesky" | custom-call | tf_op jit(solution)/shard_map/jit(cholesky)/cholesky | solution.py:61
  317.1 4.9 %custom-call.10 = f32[1,64,64]{1,2,0:T(8,128)S(1)} custom-call(f32[1,64,64]{2,1,0:T(8,128)S(1)} %fusion.68), custom_call_target="InvertDiagBlocksLowerTriangular" | custom-call | tf_op jit(solution)/shard_map/jit(_cho_solve)/triangular_solve | solution.py:62
  322.6 13.5 %fusion.57 = f32[2,8,512,128]{3,1,2,0:T(8,128)S(1)} fusion(f32[16,80]{1,0:T(8,128)S(1)} %fusion.88, f32[80,65536]{1,0:T(8,128)} %bitcast_dynamic-update-slice_fusion, f32[65536,16]{0,1:T(8,128)} %copy-done.2), kind=kOutput, calls=%fused_computation.125 | convolution fusion | flops 1007681536 | bytes 29365248 | tf_op jit(solution)/shard_map/dot_general | solution.py:94
  338.9 12.9 %fusion.54 = f32[2,8,512,128]{3,1,2,0:T(8,128)} fusion(f32[64,16]{0,1:T(8,128)S(1)} %fusion.69, f32[16,65536]{1,0:T(8,128)} %bitcast.90, f32[16,65536]{1,0:T(8,128)} %bitcast.89, f32[16,65536]{1,0:T(8,128)} %bitcast.88, f32[16,65536]{1,0:T(8,128)} %bitcast.86), kind=kOutput, calls=%fused_computation.124 | convolution fusion | flops 817889280 | bytes 20975616 | tf_op jit(solution)/shard_map/dot_general | solution.py:92
  351.8 5.0 %copy.14 = f32[2,8,512,128]{3,2,1,0:T(8,128)} copy(f32[2,8,512,128]{3,1,2,0:T(8,128)} %fusion.54) | data formatting | bytes 8388608
  (84 shorter events, 51.1 us)
Async XLA Ops:
  0.6 1.4 copy-start
  9.6 2.0 copy-start.2
  9.6 2.0 copy-start.17
  13.6 9.3 %collective-permute-start = (f32[17,1,32,128]{3,2,1,0:T(8,128)S(1)}, f32[17,1,32,128]{3,2,1,0:T(8,128)S(1)}, u32[]{:S(2)}, u32[]{:S(2)}) collective-permute-start(f32[17,1,32,128]{3,2,1,0:T(8,128)S(1)} %get-tuple-element.18), channel_id=1, source_target_pairs={{0,8},{8,16},{16,24},{24,32},{32,40},{40,48},{48,56},{56,64},{64,7... | collective-permute-start | bytes 835592 | tf_op jit(solution)/shard_map/ppermute | solution.py:20
  17.6 9.1 %collective-permute-start.1 = (f32[17,1,32,128]{3,2,1,0:T(8,128)S(1)}, f32[17,1,32,128]{3,2,1,0:T(8,128)S(1)}, u32[]{:S(2)}, u32[]{:S(2)}) collective-permute-start(f32[17,1,32,128]{3,2,1,0:T(8,128)S(1)} %get-tuple-element.19), channel_id=1, source_target_pairs={{8,0},{16,8},{24,16},{32,24},{40,32},{48,40},{56,48},{64,56},{72,6... | collective-permute-start | bytes 835592 | tf_op jit(solution)/shard_map/ppermute | solution.py:21
  22.9 16.8 %copy-start.8 = (f32[17,1,32,128]{3,2,1,0:T(8,128)}, f32[17,1,32,128]{3,2,1,0:T(8,128)S(1)}, u32[]{:S(2)}) copy-start(f32[17,1,32,128]{3,2,1,0:T(8,128)S(1)} %collective-permute-done) | copy-start | bytes 835588
  26.7 13.0 %copy-start.9 = (f32[17,1,32,128]{3,2,1,0:T(8,128)}, f32[17,1,32,128]{3,2,1,0:T(8,128)S(1)}, u32[]{:S(2)}) copy-start(f32[17,1,32,128]{3,2,1,0:T(8,128)S(1)} %collective-permute-done.1) | copy-start | bytes 835588
  26.9 7.1 %collective-permute-start.2 = (f32[17,18,1,128]{3,2,1,0:T(1,128)S(1)}, f32[17,18,1,128]{3,2,1,0:T(1,128)S(1)}, u32[]{:S(2)}, u32[]{:S(2)}) collective-permute-start(f32[17,18,1,128]{3,2,1,0:T(1,128)S(1)} %get-tuple-element.10), channel_id=1, source_target_pairs={{0,1},{1,2},{2,3},{3,4},{4,5},{5,6},{6,7},{8,9},{9,10},{10,11},{11... | collective-permute-start | bytes 470024 | tf_op jit(solution)/shard_map/ppermute | solution.py:20
  31.9 6.6 %collective-permute-start.3 = (f32[17,18,1,128]{3,2,1,0:T(1,128)S(1)}, f32[17,18,1,128]{3,2,1,0:T(1,128)S(1)}, u32[]{:S(2)}, u32[]{:S(2)}) collective-permute-start(f32[17,18,1,128]{3,2,1,0:T(1,128)S(1)} %get-tuple-element.11), channel_id=1, source_target_pairs={{1,0},{2,1},{3,2},{4,3},{5,4},{6,5},{7,6},{9,8},{10,9},{11,10},{12... | collective-permute-start | bytes 470024 | tf_op jit(solution)/shard_map/ppermute | solution.py:21
  34.1 5.6 %copy-start.12 = (f32[17,18,1,128]{3,2,1,0:T(1,128)}, f32[17,18,1,128]{3,2,1,0:T(1,128)S(1)}, u32[]{:S(2)}) copy-start(f32[17,18,1,128]{3,2,1,0:T(1,128)S(1)} %collective-permute-done.2) | copy-start | bytes 470020
  38.4 1.2 copy-start.13
  58.4 6.4 %collective-permute-start.4 = (f32[16,1,32,128]{3,2,1,0:T(8,128)S(1)}, f32[16,1,32,128]{3,2,1,0:T(8,128)S(1)}, u32[]{:S(2)}, u32[]{:S(2)}) collective-permute-start(f32[16,1,32,128]{3,2,1,0:T(8,128)S(1)} %get-tuple-element.24), channel_id=1, source_target_pairs={{0,8},{8,16},{16,24},{24,32},{32,40},{40,48},{48,56},{56,64},{64,7... | collective-permute-start | bytes 786440 | tf_op jit(solution)/shard_map/ppermute | solution.py:20
  61.5 7.4 %collective-permute-start.5 = (f32[16,1,32,128]{3,2,1,0:T(8,128)S(1)}, f32[16,1,32,128]{3,2,1,0:T(8,128)S(1)}, u32[]{:S(2)}, u32[]{:S(2)}) collective-permute-start(f32[16,1,32,128]{3,2,1,0:T(8,128)S(1)} %get-tuple-element.25), channel_id=1, source_target_pairs={{8,0},{16,8},{24,16},{32,24},{40,32},{48,40},{56,48},{64,56},{72,6... | collective-permute-start | bytes 786440 | tf_op jit(solution)/shard_map/ppermute | solution.py:21
  69.1 7.4 %collective-permute-start.6 = (f32[16,18,1,128]{3,2,1,0:T(1,128)S(1)}, f32[16,18,1,128]{3,2,1,0:T(1,128)S(1)}, u32[]{:S(2)}, u32[]{:S(2)}) collective-permute-start(f32[16,18,1,128]{3,2,1,0:T(1,128)S(1)} %get-tuple-element.16), channel_id=1, source_target_pairs={{0,1},{1,2},{2,3},{3,4},{4,5},{5,6},{6,7},{8,9},{9,10},{10,11},{11... | collective-permute-start | bytes 442376 | tf_op jit(solution)/shard_map/ppermute | solution.py:20
  74.3 15.5 %copy-start.3 = (f32[16,32,128]{2,1,0:T(8,128)S(1)}, f32[16,32,128]{2,1,0:T(8,128)}, u32[]{:S(2)}) copy-start(f32[16,32,128]{2,1,0:T(8,128)} %get-tuple-element.6) | copy-start | bytes 786436
  74.3 15.5 %copy-start.4 = (f32[16,32,128]{2,1,0:T(8,128)S(1)}, f32[16,32,128]{2,1,0:T(8,128)}, u32[]{:S(2)}) copy-start(f32[16,32,128]{2,1,0:T(8,128)} %get-tuple-element.7) | copy-start | bytes 786436
  74.3 15.5 %copy-start.6 = (f32[16,32,128]{2,1,0:T(8,128)S(1)}, f32[16,32,128]{2,1,0:T(8,128)}, u32[]{:S(2)}) copy-start(f32[16,32,128]{2,1,0:T(8,128)} %get-tuple-element.8) | copy-start | bytes 786436
  74.3 6.6 %collective-permute-start.7 = (f32[16,18,1,128]{3,2,1,0:T(1,128)S(1)}, f32[16,18,1,128]{3,2,1,0:T(1,128)S(1)}, u32[]{:S(2)}, u32[]{:S(2)}) collective-permute-start(f32[16,18,1,128]{3,2,1,0:T(1,128)S(1)} %get-tuple-element.17), channel_id=1, source_target_pairs={{1,0},{2,1},{3,2},{4,3},{5,4},{6,5},{7,6},{9,8},{10,9},{11,10},{12... | collective-permute-start | bytes 442376 | tf_op jit(solution)/shard_map/ppermute | solution.py:21
  100.7 7.8 %collective-permute-start.8 = (f32[16,1,32,128]{3,2,1,0:T(8,128)S(1)}, f32[16,1,32,128]{3,2,1,0:T(8,128)S(1)}, u32[]{:S(2)}, u32[]{:S(2)}) collective-permute-start(f32[16,1,32,128]{3,2,1,0:T(8,128)S(1)} %get-tuple-element.22), channel_id=1, source_target_pairs={{0,8},{8,16},{16,24},{24,32},{32,40},{40,48},{48,56},{56,64},{64,7... | collective-permute-start | bytes 786440 | tf_op jit(solution)/shard_map/ppermute | solution.py:20
  105.2 7.8 %collective-permute-start.9 = (f32[16,1,32,128]{3,2,1,0:T(8,128)S(1)}, f32[16,1,32,128]{3,2,1,0:T(8,128)S(1)}, u32[]{:S(2)}, u32[]{:S(2)}) collective-permute-start(f32[16,1,32,128]{3,2,1,0:T(8,128)S(1)} %get-tuple-element.23), channel_id=1, source_target_pairs={{8,0},{16,8},{24,16},{32,24},{40,32},{48,40},{56,48},{64,56},{72,6... | collective-permute-start | bytes 786440 | tf_op jit(solution)/shard_map/ppermute | solution.py:21
  108.5 20.2 %copy-start.10 = (f32[16,1,32,128]{3,2,1,0:T(8,128)}, f32[16,1,32,128]{3,2,1,0:T(8,128)S(1)}, u32[]{:S(2)}) copy-start(f32[16,1,32,128]{3,2,1,0:T(8,128)S(1)} %collective-permute-done.8) | copy-start | bytes 786436
  113.0 15.7 %copy-start.11 = (f32[16,1,32,128]{3,2,1,0:T(8,128)}, f32[16,1,32,128]{3,2,1,0:T(8,128)S(1)}, u32[]{:S(2)}) copy-start(f32[16,1,32,128]{3,2,1,0:T(8,128)S(1)} %collective-permute-done.9) | copy-start | bytes 786436
  113.2 15.5 %collective-permute-start.10 = (f32[16,18,1,128]{3,2,1,0:T(1,128)S(1)}, f32[16,18,1,128]{3,2,1,0:T(1,128)S(1)}, u32[]{:S(2)}, u32[]{:S(2)}) collective-permute-start(f32[16,18,1,128]{3,2,1,0:T(1,128)S(1)} %get-tuple-element.14), channel_id=1, source_target_pairs={{0,1},{1,2},{2,3},{3,4},{4,5},{5,6},{6,7},{8,9},{9,10},{10,11},{11... | collective-permute-start | bytes 442376 | tf_op jit(solution)/shard_map/ppermute | solution.py:20
  117.7 11.0 %collective-permute-start.11 = (f32[16,18,1,128]{3,2,1,0:T(1,128)S(1)}, f32[16,18,1,128]{3,2,1,0:T(1,128)S(1)}, u32[]{:S(2)}, u32[]{:S(2)}) collective-permute-start(f32[16,18,1,128]{3,2,1,0:T(1,128)S(1)} %get-tuple-element.15), channel_id=1, source_target_pairs={{1,0},{2,1},{3,2},{4,3},{5,4},{6,5},{7,6},{9,8},{10,9},{11,10},{12... | collective-permute-start | bytes 442376 | tf_op jit(solution)/shard_map/ppermute | solution.py:21
  128.7 10.2 %copy-start.5 = (f32[16,32,128]{2,1,0:T(8,128)S(1)}, f32[16,32,128]{2,1,0:T(8,128)}, u32[]{:S(2)}) copy-start(f32[16,32,128]{2,1,0:T(8,128)} %get-tuple-element.7) | copy-start | bytes 786436
  128.7 10.2 %copy-start.7 = (f32[16,32,128]{2,1,0:T(8,128)S(1)}, f32[16,32,128]{2,1,0:T(8,128)}, u32[]{:S(2)}) copy-start(f32[16,32,128]{2,1,0:T(8,128)} %get-tuple-element.8) | copy-start | bytes 786436
  147.0 14.3 %collective-permute-start.12 = (f32[16,1,32,128]{3,2,1,0:T(8,128)S(1)}, f32[16,1,32,128]{3,2,1,0:T(8,128)S(1)}, u32[]{:S(2)}, u32[]{:S(2)}) collective-permute-start(f32[16,1,32,128]{3,2,1,0:T(8,128)S(1)} %get-tuple-element.20), channel_id=1, source_target_pairs={{0,8},{8,16},{16,24},{24,32},{32,40},{40,48},{48,56},{56,64},{64,7... | collective-permute-start | bytes 786440 | tf_op jit(solution)/shard_map/ppermute | solution.py:20
  150.8 10.5 %collective-permute-start.13 = (f32[16,1,32,128]{3,2,1,0:T(8,128)S(1)}, f32[16,1,32,128]{3,2,1,0:T(8,128)S(1)}, u32[]{:S(2)}, u32[]{:S(2)}) collective-permute-start(f32[16,1,32,128]{3,2,1,0:T(8,128)S(1)} %get-tuple-element.21), channel_id=1, source_target_pairs={{8,0},{16,8},{24,16},{32,24},{40,32},{48,40},{56,48},{64,56},{72,6... | collective-permute-start | bytes 786440 | tf_op jit(solution)/shard_map/ppermute | solution.py:21
  161.5 14.7 %collective-permute-start.14 = (f32[16,18,1,128]{3,2,1,0:T(1,128)S(1)}, f32[16,18,1,128]{3,2,1,0:T(1,128)S(1)}, u32[]{:S(2)}, u32[]{:S(2)}) collective-permute-start(f32[16,18,1,128]{3,2,1,0:T(1,128)S(1)} %get-tuple-element.12), channel_id=1, source_target_pairs={{0,1},{1,2},{2,3},{3,4},{4,5},{5,6},{6,7},{8,9},{9,10},{10,11},{11... | collective-permute-start | bytes 442376 | tf_op jit(solution)/shard_map/ppermute | solution.py:20
  165.5 10.7 %collective-permute-start.15 = (f32[16,18,1,128]{3,2,1,0:T(1,128)S(1)}, f32[16,18,1,128]{3,2,1,0:T(1,128)S(1)}, u32[]{:S(2)}, u32[]{:S(2)}) collective-permute-start(f32[16,18,1,128]{3,2,1,0:T(1,128)S(1)} %get-tuple-element.13), channel_id=1, source_target_pairs={{1,0},{2,1},{3,2},{4,3},{5,4},{6,5},{7,6},{9,8},{10,9},{11,10},{12... | collective-permute-start | bytes 442376 | tf_op jit(solution)/shard_map/ppermute | solution.py:21
  200.5 108.7 %copy-start.14 = (f32[80,64]{1,0:T(8,128)S(1)}, f32[80,64]{1,0:T(8,128)}, u32[]{:S(2)}) copy-start(f32[80,64]{1,0:T(8,128)} %constant.62.clone) | copy-start | bytes 61444
  338.9 17.9 %copy-start.1 = (f32[16,64]{1,0:T(8,128)S(1)}, f32[16,64]{1,0:T(8,128)}, u32[]{:S(2)}) copy-start(f32[16,64]{1,0:T(8,128)} %param.10) | copy-start | bytes 12292
  (2 other events, 1.3 us)
where the time goes:
time: 364 us; the launch traced here: 357 us
  other arithmetic  91.4 us (25%)
  blocking collectives  85.6 us (24%)
  matrix products  58.2 us (16%)
  starting transfers between devices  47.6 us (13%)
  local copies, waits for them, and re-layouts  43.6 us (12%)
  waiting for transfers between devices  29.4 us (8%)
    psum x1, blocking collectives, shards(): gram = lax.psum(jnp.dot(flat, flat.T, precision=highest), ('gx', 'gy'))  85.6 us
    select_n x4, other arithmetic, neighbour_mean(): jnp.where(inside[None], summed / jnp.where(inside, weights, 1.0)[None], 0.0)  38.9 us
    unnamed x45, local copies, waits for them, and re-layouts  37.6 us
    concatenate x4, other arithmetic, with_halo(): value = jnp.concatenate([before, value, after], axis=dim)  36.4 us
    ppermute x8, starting transfers between devices, with_halo(): before = lax.ppermute(last, axis, up)  33.9 us
    dot_general x1, matrix products, shards(): gram = lax.psum(jnp.dot(flat, flat.T, precision=highest), ('gx', 'gy'))  23 us
    ppermute x8, waiting for transfers between devices, with_halo(): after = lax.ppermute(initial, axis, down)  21.1 us
    ppermute x8, starting transfers between devices, with_halo(): after = lax.ppermute(initial, axis, down)  13.8 us
  transfers between devices with their start and end apart: 16, of which 9 were waited for; matrix products, arithmetic and copies ran while one was open for 7% of the time, Pallas kernels for 0%

commit v1 on v0

--- a/solution.py
+++ b/solution.py
@@ -87,7 +87,7 @@
         current = neighbour_mean(padded, conduct_wide)
         krylov.append(current)
     flat = jnp.concatenate([field.reshape(NRHS, -1) for field in krylov], 0)
-    gram = lax.psum(jnp.dot(flat, flat.T, precision=highest), ("gx", "gy"))
+    gram = lax.psum(lax.psum(jnp.dot(flat, flat.T, precision=highest), "gy"), "gx")
     diff, coeffs = least_squares(gram)
     solution = jnp.dot(coeffs.T, flat[: S * NRHS], precision=highest)
     combined = jnp.dot(diff, coeffs, precision=highest)

time: 364 us -> 450 us (1.24)
  the two profiles are of different devices: /device:TPU:1 before, /device:TPU:128 now
where the time goes in v1:
time: 450 us; the launch traced here: 443 us
  blocking collectives  168 us (37%)
  other arithmetic  91.4 us (20%)
  starting transfers between devices  59.6 us (13%)
  matrix products  58.2 us (13%)
  local copies, waits for them, and re-layouts  43.5 us (10%)
  waiting for transfers between devices  21 us (5%)
    psum x1, blocking collectives, shards(): lax.psum(lax.psum(jnp.dot(flat, flat.T, precision=highest), 'gy'), 'gx')  140 us
    select_n x4, other arithmetic, neighbour_mean(): jnp.where(inside[None], summed / jnp.where(inside, weights, 1.0)[None], 0.0)  39 us
    unnamed x45, local copies, waits for them, and re-layouts  37.6 us
    concatenate x4, other arithmetic, with_halo(): value = jnp.concatenate([before, value, after], axis=dim)  36.4 us
    ppermute x8, starting transfers between devices, with_halo(): after = lax.ppermute(initial, axis, down)  34.6 us
    psum x1, blocking collectives, shards(): lax.psum(jnp.dot(flat, flat.T, precision=highest), 'gy')  27.4 us
    ppermute x8, starting transfers between devices, with_halo(): before = lax.ppermute(last, axis, up)  25 us
    dot_general x1, matrix products, shards(): jnp.dot(flat, flat.T, precision=highest)  23 us
  transfers between devices with their start and end apart: 16, of which 8 were waited for; matrix products, arithmetic and copies ran while one was open for 6% of the time, Pallas kernels for 0%

profile of v1, /device:TPU:128, one launch (start us, length us, event | category | flops | bytes accessed | tf_op | source)
XLA Modules:
  0.0 442.5 jit_solution(17588083081270935633)
XLA Ops:
  2.0 7.5 %constant_dynamic-update-slice_fusion.3 = (f32[80,65536]{1,0:T(8,128)}, f32[65536,16]{0,1:T(8,128)S(1)}) fusion(f32[65536]{0:T(1024)} %bitcast.93, f32[16,64]{1,0:T(8,128)S(1)} %copy-done, s32[65536]{0:T(1024)} %bitcast.94), kind=kOutput, calls=%fused_computation.175 | convolution fusion | flops 810549248 | bytes 8916992 | tf_op jit(solution)/shard_map/dot_general | solution.py:77
  16.9 5.8 %collective-permute-start.1 = (f32[17,1,32,128]{3,2,1,0:T(8,128)S(1)}, f32[17,1,32,128]{3,2,1,0:T(8,128)S(1)}, u32[]{:S(2)}, u32[]{:S(2)}) collective-permute-start(f32[17,1,32,128]{3,2,1,0:T(8,128)S(1)} %get-tuple-element.19), channel_id=1, source_target_pairs={{8,0},{16,8},{24,16},{32,24},{40,32},{48,40},{56,48},{64,56},{72,6... | collective-permute-start | bytes 835592 | tf_op jit(solution)/shard_map/ppermute | solution.py:21
  22.7 4.4 %collective-permute-done = f32[17,1,32,128]{3,2,1,0:T(8,128)S(1)} collective-permute-done((f32[17,1,32,128]{3,2,1,0:T(8,128)S(1)}, f32[17,1,32,128]{3,2,1,0:T(8,128)S(1)}, u32[]{:S(2)}, u32[]{:S(2)}) %collective-permute-start) | collective-permute-done | bytes 278560 | tf_op jit(solution)/shard_map/ppermute | solution.py:20
  36.1 9.7 %select_maximum_fusion.12 = f32[16,18,34,130]{3,2,1,0:T(8,128)} fusion(f32[17,18,1,128]{3,2,1,0:T(1,128)S(1)} %collective-permute-done.3, f32[17,18,1,128]{3,2,1,0:T(1,128)S(1)} %collective-permute-done.2, f32[17,1,32,128]{3,2,1,0:T(8,128)S(1)} %collective-permute-done.1, f32[17,1,32,128]{3,2,1,0:T(8,128)S(1)} %collective-permute-done, ...), kind=kLoop, calls=%fused_computation.25 | loop fusion | flops 17821440 | bytes 10418688 | tf_op jit(solution)/shard_map/concatenate | solution.py:22
  45.8 9.0 %fusion.45 = f32[16,16,32,128]{3,2,1,0:T(8,128)S(1)} fusion(f32[16,18,34,130]{3,2,1,0:T(8,128)} %select_maximum_fusion.12, f32[17,18,1,128]{3,2,1,0:T(1,128)} %copy-done.13, f32[17,1,32,128]{3,2,1,0:T(8,128)} %copy-done.9, f32[17,1,32,128]{3,2,1,0:T(8,128)} %copy-done.8, f32[16,16,32,128]{3,2,1,0:T(8,128)S(1)} %bitcast.84, ...), kind=kLoop, calls=%fused_computation.102 | loop fusion | flops 26214400 | bytes 19810304 | tf_op jit(solution)/shard_map/jit(_where)/select_n | solution.py:44
  56.9 7.6 %collective-permute-start.5 = (f32[16,1,32,128]{3,2,1,0:T(8,128)S(1)}, f32[16,1,32,128]{3,2,1,0:T(8,128)S(1)}, u32[]{:S(2)}, u32[]{:S(2)}) collective-permute-start(f32[16,1,32,128]{3,2,1,0:T(8,128)S(1)} %get-tuple-element.25), channel_id=1, source_target_pairs={{8,0},{16,8},{24,16},{32,24},{40,32},{48,40},{56,48},{64,56},{72,6... | collective-permute-start | bytes 786440 | tf_op jit(solution)/shard_map/ppermute | solution.py:21
  68.6 4.8 %collective-permute-start.6 = (f32[16,18,1,128]{3,2,1,0:T(1,128)S(1)}, f32[16,18,1,128]{3,2,1,0:T(1,128)S(1)}, u32[]{:S(2)}, u32[]{:S(2)}) collective-permute-start(f32[16,18,1,128]{3,2,1,0:T(1,128)S(1)} %get-tuple-element.16), channel_id=1, source_target_pairs={{0,1},{1,2},{2,3},{3,4},{4,5},{5,6},{6,7},{8,9},{9,10},{10,11},{11... | collective-permute-start | bytes 442376 | tf_op jit(solution)/shard_map/ppermute | solution.py:20
  79.0 8.9 %select_maximum_fusion.8 = f32[16,18,34,130]{3,2,1,0:T(8,128)} fusion(f32[16,18,1,128]{3,2,1,0:T(1,128)S(1)} %collective-permute-done.7, f32[16,18,1,128]{3,2,1,0:T(1,128)S(1)} %collective-permute-done.6, f32[16,1,32,128]{3,2,1,0:T(8,128)S(1)} %collective-permute-done.5, f32[16,16,32,128]{3,2,1,0:T(8,128)S(1)} %fusion.45, ...), kind=kLoop, calls=%fused_computation.21 | loop fusion | flops 15275520 | bytes 10105344 | tf_op jit(solution)/shard_map/concatenate | solution.py:22
  87.9 10.9 %fusion.34 = f32[16,16,32,128]{3,2,1,0:T(8,128)S(1)} fusion(f32[16,18,34,130]{3,2,1,0:T(8,128)} %select_maximum_fusion.8, f32[16,18,1,128]{3,2,1,0:T(1,128)S(1)} %collective-permute-done.7, f32[16,1,32,128]{3,2,1,0:T(8,128)S(1)} %collective-permute-done.5, f32[16,16,32,128]{3,2,1,0:T(8,128)S(1)} %fusion.45, ...), kind=kLoop, calls=%fused_computation.81 | loop fusion | flops 22020096 | bytes 19496960 | tf_op jit(solution)/shard_map/jit(_where)/select_n | solution.py:44
  100.7 7.7 %collective-permute-start.9 = (f32[16,1,32,128]{3,2,1,0:T(8,128)S(1)}, f32[16,1,32,128]{3,2,1,0:T(8,128)S(1)}, u32[]{:S(2)}, u32[]{:S(2)}) collective-permute-start(f32[16,1,32,128]{3,2,1,0:T(8,128)S(1)} %get-tuple-element.23), channel_id=1, source_target_pairs={{8,0},{16,8},{24,16},{32,24},{40,32},{48,40},{56,48},{64,56},{72,6... | collective-permute-start | bytes 786440 | tf_op jit(solution)/shard_map/ppermute | solution.py:21
  112.5 4.8 %collective-permute-start.10 = (f32[16,18,1,128]{3,2,1,0:T(1,128)S(1)}, f32[16,18,1,128]{3,2,1,0:T(1,128)S(1)}, u32[]{:S(2)}, u32[]{:S(2)}) collective-permute-start(f32[16,18,1,128]{3,2,1,0:T(1,128)S(1)} %get-tuple-element.14), channel_id=1, source_target_pairs={{0,1},{1,2},{2,3},{3,4},{4,5},{5,6},{6,7},{8,9},{9,10},{10,11},{11... | collective-permute-start | bytes 442376 | tf_op jit(solution)/shard_map/ppermute | solution.py:20
  118.9 4.5 %constant_dynamic-update-slice_fusion.2 = f32[80,65536]{1,0:T(8,128)} fusion(f32[80,65536]{1,0:T(8,128)} %get-tuple-element.29, f32[2,8,512,128]{3,2,1,0:T(8,128)S(1)} %bitcast.74), kind=kLoop, calls=%fused_computation.174 | loop fusion | bytes 8388608
  123.3 4.4 copy.28
  129.0 8.9 %select_maximum_fusion.4 = f32[16,18,34,130]{3,2,1,0:T(8,128)} fusion(f32[16,18,1,128]{3,2,1,0:T(1,128)S(1)} %collective-permute-done.11, f32[16,18,1,128]{3,2,1,0:T(1,128)S(1)} %collective-permute-done.10, f32[16,1,32,128]{3,2,1,0:T(8,128)S(1)} %collective-permute-done.9, f32[16,16,32,128]{3,2,1,0:T(8,128)S(1)} %fusion.34, ...), kind=kLoop, calls=%fused_computation.17 | loop fusion | flops 15275520 | bytes 10105344 | tf_op jit(solution)/shard_map/concatenate | solution.py:22
  137.9 8.2 %fusion.23 = f32[16,16,32,128]{3,2,1,0:T(8,128)S(1)} fusion(f32[16,18,34,130]{3,2,1,0:T(8,128)} %select_maximum_fusion.4, f32[16,18,1,128]{3,2,1,0:T(1,128)} %copy-done.16, f32[16,1,32,128]{3,2,1,0:T(8,128)} %copy-done.11, f32[16,16,32,128]{3,2,1,0:T(8,128)S(1)} %fusion.34, f32[16,1,32,128]{3,2,1,0:T(8,128)} %copy-done.10, f32[16,18,1,128]{3,2,1,0:T(1,128)} %copy-done.15, ...), kind=kLoop, calls=%fused_computation.60 | loop fusion | flops 22020096 | bytes 19496960 | tf_op jit(solution)/shard_map/jit(_where)/select_n | solution.py:44
  148.0 7.8 %collective-permute-start.13 = (f32[16,1,32,128]{3,2,1,0:T(8,128)S(1)}, f32[16,1,32,128]{3,2,1,0:T(8,128)S(1)}, u32[]{:S(2)}, u32[]{:S(2)}) collective-permute-start(f32[16,1,32,128]{3,2,1,0:T(8,128)S(1)} %get-tuple-element.21), channel_id=1, source_target_pairs={{8,0},{16,8},{24,16},{32,24},{40,32},{48,40},{56,48},{64,56},{72,6... | collective-permute-start | bytes 786440 | tf_op jit(solution)/shard_map/ppermute | solution.py:21
  155.9 4.4 %constant_dynamic-update-slice_fusion.1 = f32[80,65536]{1,0:T(8,128)} fusion(f32[80,65536]{1,0:T(8,128)} %constant_dynamic-update-slice_fusion.2, f32[2,8,512,128]{3,2,1,0:T(8,128)S(1)} %bitcast.76), kind=kLoop, calls=%fused_computation.173 | loop fusion | bytes 8388608
  160.3 4.4 copy.27
  164.9 4.8 %collective-permute-start.14 = (f32[16,18,1,128]{3,2,1,0:T(1,128)S(1)}, f32[16,18,1,128]{3,2,1,0:T(1,128)S(1)}, u32[]{:S(2)}, u32[]{:S(2)}) collective-permute-start(f32[16,18,1,128]{3,2,1,0:T(1,128)S(1)} %get-tuple-element.12), channel_id=1, source_target_pairs={{0,1},{1,2},{2,3},{3,4},{4,5},{5,6},{6,7},{8,9},{9,10},{10,11},{11... | collective-permute-start | bytes 442376 | tf_op jit(solution)/shard_map/ppermute | solution.py:20
  170.9 4.4 constant_dynamic-update-slice_fusion
  175.3 4.4 %copy.26 = f32[2,8,512,128]{3,1,2,0:T(8,128)} copy(f32[2,8,512,128]{3,2,1,0:T(8,128)S(1)} %bitcast.79) | data formatting | bytes 8388608
  179.8 9.0 %select_maximum_fusion = f32[16,18,34,130]{3,2,1,0:T(8,128)} fusion(f32[16,18,1,128]{3,2,1,0:T(1,128)S(1)} %collective-permute-done.15, f32[16,18,1,128]{3,2,1,0:T(1,128)S(1)} %collective-permute-done.14, f32[16,1,32,128]{3,2,1,0:T(8,128)S(1)} %collective-permute-done.13, f32[16,16,32,128]{3,2,1,0:T(8,128)S(1)} %fusion.23, ...), kind=kLoop, calls=%fused_computation.13 | loop fusion | flops 15275520 | bytes 10105344 | tf_op jit(solution)/shard_map/concatenate | solution.py:22
  188.8 10.9 %fusion.12 = f32[16,16,32,128]{3,2,1,0:T(8,128)S(1)} fusion(f32[16,18,34,130]{3,2,1,0:T(8,128)} %select_maximum_fusion, f32[16,18,1,128]{3,2,1,0:T(1,128)S(1)} %collective-permute-done.15, f32[16,1,32,128]{3,2,1,0:T(8,128)S(1)} %collective-permute-done.13, f32[16,16,32,128]{3,2,1,0:T(8,128)S(1)} %fusion.23, ...), kind=kLoop, calls=%fused_computation.39 | loop fusion | flops 22020096 | bytes 19496960 | tf_op jit(solution)/shard_map/jit(_where)/select_n | solution.py:44
  199.7 4.4 bitcast_dynamic-update-slice_fusion
  204.1 23.0 %fusion.85 = f32[80,80]{1,0:T(8,128)S(1)} fusion(f32[80,65536]{1,0:T(8,128)} %bitcast_dynamic-update-slice_fusion), kind=kOutput, calls=%fused_computation.182 | convolution fusion | flops 5033164800 | bytes 20997120 | tf_op jit(solution)/shard_map/dot_general | solution.py:90
  227.1 27.4 %psum.14 = f32[80,80]{1,0:T(8,128)S(1)} all-reduce(f32[80,80]{1,0:T(8,128)S(1)} %fusion.85), channel_id=1, replica_groups=mesh['gx'=32,'gy'=8] {'gy'}, use_global_device_ids=true, to_apply=%region_0.1 | all-reduce | flops 6400 | bytes 51200 | tf_op jit(solution)/shard_map/psum | solution.py:90
  254.4 140.2 %psum.15 = f32[80,80]{1,0:T(8,128)S(1)} all-reduce(f32[80,80]{1,0:T(8,128)S(1)} %psum.14), channel_id=1, replica_groups=mesh['gx'=32,'gy'=8] {'gx'}, use_global_device_ids=true, to_apply=%region_1.2 | all-reduce | flops 6400 | bytes 51200 | tf_op jit(solution)/shard_map/psum | solution.py:90
  395.4 5.8 %cholesky.16 = f32[64,64]{1,0:T(8,128)S(1)} custom-call(f32[64,64]{1,0:T(8,128)S(1)} %fusion.73), custom_call_target="Cholesky" | custom-call | tf_op jit(solution)/shard_map/jit(cholesky)/cholesky | solution.py:61
  402.6 4.9 %custom-call.10 = f32[1,64,64]{1,2,0:T(8,128)S(1)} custom-call(f32[1,64,64]{2,1,0:T(8,128)S(1)} %fusion.68), custom_call_target="InvertDiagBlocksLowerTriangular" | custom-call | tf_op jit(solution)/shard_map/jit(_cho_solve)/triangular_solve | solution.py:62
  408.1 13.5 %fusion.57 = f32[2,8,512,128]{3,1,2,0:T(8,128)S(1)} fusion(f32[16,80]{1,0:T(8,128)S(1)} %fusion.88, f32[80,65536]{1,0:T(8,128)} %bitcast_dynamic-update-slice_fusion, f32[65536,16]{0,1:T(8,128)} %copy-done.2), kind=kOutput, calls=%fused_computation.125 | convolution fusion | flops 1007681536 | bytes 29365248 | tf_op jit(solution)/shard_map/dot_general | solution.py:94
  424.4 12.9 %fusion.54 = f32[2,8,512,128]{3,1,2,0:T(8,128)} fusion(f32[64,16]{0,1:T(8,128)S(1)} %fusion.69, f32[16,65536]{1,0:T(8,128)} %bitcast.90, f32[16,65536]{1,0:T(8,128)} %bitcast.89, f32[16,65536]{1,0:T(8,128)} %bitcast.88, f32[16,65536]{1,0:T(8,128)} %bitcast.86), kind=kOutput, calls=%fused_computation.124 | convolution fusion | flops 817889280 | bytes 20975616 | tf_op jit(solution)/shard_map/dot_general | solution.py:92
  437.3 5.0 %copy.14 = f32[2,8,512,128]{3,2,1,0:T(8,128)} copy(f32[2,8,512,128]{3,1,2,0:T(8,128)} %fusion.54) | data formatting | bytes 8388608
  (85 shorter events, 47.1 us)
Async XLA Ops:
  0.6 1.4 copy-start
  9.5 2.0 copy-start.2
  9.5 2.0 copy-start.17
  13.5 13.6 %collective-permute-start = (f32[17,1,32,128]{3,2,1,0:T(8,128)S(1)}, f32[17,1,32,128]{3,2,1,0:T(8,128)S(1)}, u32[]{:S(2)}, u32[]{:S(2)}) collective-permute-start(f32[17,1,32,128]{3,2,1,0:T(8,128)S(1)} %get-tuple-element.18), channel_id=1, source_target_pairs={{0,8},{8,16},{16,24},{24,32},{32,40},{40,48},{48,56},{56,64},{64,7... | collective-permute-start | bytes 835592 | tf_op jit(solution)/shard_map/ppermute | solution.py:20
  16.9 11.4 %collective-permute-start.1 = (f32[17,1,32,128]{3,2,1,0:T(8,128)S(1)}, f32[17,1,32,128]{3,2,1,0:T(8,128)S(1)}, u32[]{:S(2)}, u32[]{:S(2)}) collective-permute-start(f32[17,1,32,128]{3,2,1,0:T(8,128)S(1)} %get-tuple-element.19), channel_id=1, source_target_pairs={{8,0},{16,8},{24,16},{32,24},{40,32},{48,40},{56,48},{64,56},{72,6... | collective-permute-start | bytes 835592 | tf_op jit(solution)/shard_map/ppermute | solution.py:21
  27.1 9.0 %copy-start.8 = (f32[17,1,32,128]{3,2,1,0:T(8,128)}, f32[17,1,32,128]{3,2,1,0:T(8,128)S(1)}, u32[]{:S(2)}) copy-start(f32[17,1,32,128]{3,2,1,0:T(8,128)S(1)} %collective-permute-done) | copy-start | bytes 835588
  28.3 7.8 %copy-start.9 = (f32[17,1,32,128]{3,2,1,0:T(8,128)}, f32[17,1,32,128]{3,2,1,0:T(8,128)S(1)}, u32[]{:S(2)}) copy-start(f32[17,1,32,128]{3,2,1,0:T(8,128)S(1)} %collective-permute-done.1) | copy-start | bytes 835588
  28.5 2.6 collective-permute-start.2
  29.8 5.1 %collective-permute-start.3 = (f32[17,18,1,128]{3,2,1,0:T(1,128)S(1)}, f32[17,18,1,128]{3,2,1,0:T(1,128)S(1)}, u32[]{:S(2)}, u32[]{:S(2)}) collective-permute-start(f32[17,18,1,128]{3,2,1,0:T(1,128)S(1)} %get-tuple-element.11), channel_id=1, source_target_pairs={{1,0},{2,1},{3,2},{4,3},{5,4},{6,5},{7,6},{9,8},{10,9},{11,10},{12... | collective-permute-start | bytes 470024 | tf_op jit(solution)/shard_map/ppermute | solution.py:21
  31.1 5.0 %copy-start.12 = (f32[17,18,1,128]{3,2,1,0:T(1,128)}, f32[17,18,1,128]{3,2,1,0:T(1,128)S(1)}, u32[]{:S(2)}) copy-start(f32[17,18,1,128]{3,2,1,0:T(1,128)S(1)} %collective-permute-done.2) | copy-start | bytes 470020
  34.9 1.2 copy-start.13
  54.9 12.1 %collective-permute-start.4 = (f32[16,1,32,128]{3,2,1,0:T(8,128)S(1)}, f32[16,1,32,128]{3,2,1,0:T(8,128)S(1)}, u32[]{:S(2)}, u32[]{:S(2)}) collective-permute-start(f32[16,1,32,128]{3,2,1,0:T(8,128)S(1)} %get-tuple-element.24), channel_id=1, source_target_pairs={{0,8},{8,16},{16,24},{24,32},{32,40},{40,48},{48,56},{56,64},{64,7... | collective-permute-start | bytes 786440 | tf_op jit(solution)/shard_map/ppermute | solution.py:20
  56.9 11.5 %collective-permute-start.5 = (f32[16,1,32,128]{3,2,1,0:T(8,128)S(1)}, f32[16,1,32,128]{3,2,1,0:T(8,128)S(1)}, u32[]{:S(2)}, u32[]{:S(2)}) collective-permute-start(f32[16,1,32,128]{3,2,1,0:T(8,128)S(1)} %get-tuple-element.25), channel_id=1, source_target_pairs={{8,0},{16,8},{24,16},{32,24},{40,32},{48,40},{56,48},{64,56},{72,6... | collective-permute-start | bytes 786440 | tf_op jit(solution)/shard_map/ppermute | solution.py:21
  68.6 6.5 %collective-permute-start.6 = (f32[16,18,1,128]{3,2,1,0:T(1,128)S(1)}, f32[16,18,1,128]{3,2,1,0:T(1,128)S(1)}, u32[]{:S(2)}, u32[]{:S(2)}) collective-permute-start(f32[16,18,1,128]{3,2,1,0:T(1,128)S(1)} %get-tuple-element.16), channel_id=1, source_target_pairs={{0,1},{1,2},{2,3},{3,4},{4,5},{5,6},{6,7},{8,9},{9,10},{10,11},{11... | collective-permute-start | bytes 442376 | tf_op jit(solution)/shard_map/ppermute | solution.py:20
  73.4 14.4 %copy-start.3 = (f32[16,32,128]{2,1,0:T(8,128)S(1)}, f32[16,32,128]{2,1,0:T(8,128)}, u32[]{:S(2)}) copy-start(f32[16,32,128]{2,1,0:T(8,128)} %get-tuple-element.6) | copy-start | bytes 786436
  73.4 14.4 %copy-start.4 = (f32[16,32,128]{2,1,0:T(8,128)S(1)}, f32[16,32,128]{2,1,0:T(8,128)}, u32[]{:S(2)}) copy-start(f32[16,32,128]{2,1,0:T(8,128)} %get-tuple-element.7) | copy-start | bytes 786436
  73.5 14.4 %copy-start.6 = (f32[16,32,128]{2,1,0:T(8,128)S(1)}, f32[16,32,128]{2,1,0:T(8,128)}, u32[]{:S(2)}) copy-start(f32[16,32,128]{2,1,0:T(8,128)} %get-tuple-element.8) | copy-start | bytes 786436
  73.5 5.5 %collective-permute-start.7 = (f32[16,18,1,128]{3,2,1,0:T(1,128)S(1)}, f32[16,18,1,128]{3,2,1,0:T(1,128)S(1)}, u32[]{:S(2)}, u32[]{:S(2)}) collective-permute-start(f32[16,18,1,128]{3,2,1,0:T(1,128)S(1)} %get-tuple-element.17), channel_id=1, source_target_pairs={{1,0},{2,1},{3,2},{4,3},{5,4},{6,5},{7,6},{9,8},{10,9},{11,10},{12... | collective-permute-start | bytes 442376 | tf_op jit(solution)/shard_map/ppermute | solution.py:21
  98.8 12.1 %collective-permute-start.8 = (f32[16,1,32,128]{3,2,1,0:T(8,128)S(1)}, f32[16,1,32,128]{3,2,1,0:T(8,128)S(1)}, u32[]{:S(2)}, u32[]{:S(2)}) collective-permute-start(f32[16,1,32,128]{3,2,1,0:T(8,128)S(1)} %get-tuple-element.22), channel_id=1, source_target_pairs={{0,8},{8,16},{16,24},{24,32},{32,40},{40,48},{48,56},{56,64},{64,7... | collective-permute-start | bytes 786440 | tf_op jit(solution)/shard_map/ppermute | solution.py:20
  100.7 11.6 %collective-permute-start.9 = (f32[16,1,32,128]{3,2,1,0:T(8,128)S(1)}, f32[16,1,32,128]{3,2,1,0:T(8,128)S(1)}, u32[]{:S(2)}, u32[]{:S(2)}) collective-permute-start(f32[16,1,32,128]{3,2,1,0:T(8,128)S(1)} %get-tuple-element.23), channel_id=1, source_target_pairs={{8,0},{16,8},{24,16},{32,24},{40,32},{48,40},{56,48},{64,56},{72,6... | collective-permute-start | bytes 786440 | tf_op jit(solution)/shard_map/ppermute | solution.py:21
  110.9 16.9 %copy-start.10 = (f32[16,1,32,128]{3,2,1,0:T(8,128)}, f32[16,1,32,128]{3,2,1,0:T(8,128)S(1)}, u32[]{:S(2)}) copy-start(f32[16,1,32,128]{3,2,1,0:T(8,128)S(1)} %collective-permute-done.8) | copy-start | bytes 786436
  112.3 15.4 %copy-start.11 = (f32[16,1,32,128]{3,2,1,0:T(8,128)}, f32[16,1,32,128]{3,2,1,0:T(8,128)S(1)}, u32[]{:S(2)}) copy-start(f32[16,1,32,128]{3,2,1,0:T(8,128)S(1)} %collective-permute-done.9) | copy-start | bytes 786436
  112.5 15.2 %collective-permute-start.10 = (f32[16,18,1,128]{3,2,1,0:T(1,128)S(1)}, f32[16,18,1,128]{3,2,1,0:T(1,128)S(1)}, u32[]{:S(2)}, u32[]{:S(2)}) collective-permute-start(f32[16,18,1,128]{3,2,1,0:T(1,128)S(1)} %get-tuple-element.14), channel_id=1, source_target_pairs={{0,1},{1,2},{2,3},{3,4},{4,5},{5,6},{6,7},{8,9},{9,10},{10,11},{11... | collective-permute-start | bytes 442376 | tf_op jit(solution)/shard_map/ppermute | solution.py:20
  117.4 10.3 %collective-permute-start.11 = (f32[16,18,1,128]{3,2,1,0:T(1,128)S(1)}, f32[16,18,1,128]{3,2,1,0:T(1,128)S(1)}, u32[]{:S(2)}, u32[]{:S(2)}) collective-permute-start(f32[16,18,1,128]{3,2,1,0:T(1,128)S(1)} %get-tuple-element.15), channel_id=1, source_target_pairs={{1,0},{2,1},{3,2},{4,3},{5,4},{6,5},{7,6},{9,8},{10,9},{11,10},{12... | collective-permute-start | bytes 442376 | tf_op jit(solution)/shard_map/ppermute | solution.py:21
  127.7 10.2 %copy-start.5 = (f32[16,32,128]{2,1,0:T(8,128)S(1)}, f32[16,32,128]{2,1,0:T(8,128)}, u32[]{:S(2)}) copy-start(f32[16,32,128]{2,1,0:T(8,128)} %get-tuple-element.7) | copy-start | bytes 786436
  127.7 10.2 %copy-start.7 = (f32[16,32,128]{2,1,0:T(8,128)S(1)}, f32[16,32,128]{2,1,0:T(8,128)}, u32[]{:S(2)}) copy-start(f32[16,32,128]{2,1,0:T(8,128)} %get-tuple-element.8) | copy-start | bytes 786436
  146.1 18.6 %collective-permute-start.12 = (f32[16,1,32,128]{3,2,1,0:T(8,128)S(1)}, f32[16,1,32,128]{3,2,1,0:T(8,128)S(1)}, u32[]{:S(2)}, u32[]{:S(2)}) collective-permute-start(f32[16,1,32,128]{3,2,1,0:T(8,128)S(1)} %get-tuple-element.20), channel_id=1, source_target_pairs={{0,8},{8,16},{16,24},{24,32},{32,40},{40,48},{48,56},{56,64},{64,7... | collective-permute-start | bytes 786440 | tf_op jit(solution)/shard_map/ppermute | solution.py:20
  148.0 16.6 %collective-permute-start.13 = (f32[16,1,32,128]{3,2,1,0:T(8,128)S(1)}, f32[16,1,32,128]{3,2,1,0:T(8,128)S(1)}, u32[]{:S(2)}, u32[]{:S(2)}) collective-permute-start(f32[16,1,32,128]{3,2,1,0:T(8,128)S(1)} %get-tuple-element.21), channel_id=1, source_target_pairs={{8,0},{16,8},{24,16},{32,24},{40,32},{48,40},{56,48},{64,56},{72,6... | collective-permute-start | bytes 786440 | tf_op jit(solution)/shard_map/ppermute | solution.py:21
  164.9 14.9 %collective-permute-start.14 = (f32[16,18,1,128]{3,2,1,0:T(1,128)S(1)}, f32[16,18,1,128]{3,2,1,0:T(1,128)S(1)}, u32[]{:S(2)}, u32[]{:S(2)}) collective-permute-start(f32[16,18,1,128]{3,2,1,0:T(1,128)S(1)} %get-tuple-element.12), channel_id=1, source_target_pairs={{0,1},{1,2},{2,3},{3,4},{4,5},{5,6},{6,7},{8,9},{9,10},{10,11},{11... | collective-permute-start | bytes 442376 | tf_op jit(solution)/shard_map/ppermute | solution.py:20
  169.6 10.1 %collective-permute-start.15 = (f32[16,18,1,128]{3,2,1,0:T(1,128)S(1)}, f32[16,18,1,128]{3,2,1,0:T(1,128)S(1)}, u32[]{:S(2)}, u32[]{:S(2)}) collective-permute-start(f32[16,18,1,128]{3,2,1,0:T(1,128)S(1)} %get-tuple-element.13), channel_id=1, source_target_pairs={{1,0},{2,1},{3,2},{4,3},{5,4},{6,5},{7,6},{9,8},{10,9},{11,10},{12... | collective-permute-start | bytes 442376 | tf_op jit(solution)/shard_map/ppermute | solution.py:21
  204.1 190.6 %copy-start.14 = (f32[80,64]{1,0:T(8,128)S(1)}, f32[80,64]{1,0:T(8,128)}, u32[]{:S(2)}) copy-start(f32[80,64]{1,0:T(8,128)} %constant.62.clone) | copy-start | bytes 61444
  424.4 17.9 %copy-start.1 = (f32[16,64]{1,0:T(8,128)S(1)}, f32[16,64]{1,0:T(8,128)}, u32[]{:S(2)}) copy-start(f32[16,64]{1,0:T(8,128)} %param.10) | copy-start | bytes 12292
  (2 other events, 1.3 us)
